TPU v7x, 32 devices: a whole 2x2x4 slice. The times are simulated.
32 devices in a mesh: dp: 8 (over z, y), mp: 4 (over x, core).
Axes of the slice: x: 2, y: 2, z: 4, core: 2. Of those that a mesh axis runs over, the one named last changes fastest.
Arguments:
- tokens: bfloat16 [4096, 1152], P(('dp', 'mp')), may hold values from -6 to 6
- segment_ids: int32 [4096], P('dp'), may hold values from 0 to 2, as said below
- positions: int32 [4096], P('dp'), may hold values from 0 to 5118, as said below
- q_weight: bfloat16 [1152, 1024], P('dp', 'mp'), may hold values from -0.1875 to 0.1875
- kv_weight: bfloat16 [1152, 512], P('dp'), may hold values from -0.1875 to 0.1875
- o_weight: bfloat16 [1024, 1152], P('mp', 'dp'), may hold values from -0.1875 to 0.1875
- gate_up_weight: bfloat16 [2, 1152, 6912], P(None, 'dp', 'mp'), may hold values from -0.1875 to 0.1875
- down_weight: bfloat16 [6912, 1152], P('mp', 'dp'), may hold values from -0.078125 to 0.078125
- attn_pre_gain: bfloat16 [1152], P('dp'), may hold values from 0.25 to 1.75
- attn_post_gain: bfloat16 [1152], P('dp'), may hold values from 0.25 to 1.75
- ff_pre_gain: bfloat16 [1152], P('dp'), may hold values from 0.25 to 1.75
- ff_post_gain: bfloat16 [1152], P('dp'), may hold values from 0.25 to 1.75
- query_gain: bfloat16 [256], P('dp'), may hold values from 0.25 to 1.75
- key_gain: bfloat16 [256], P('dp'), may hold values from 0.25 to 1.75
- out_grad: bfloat16 [4096, 1152], P(('dp', 'mp')), may hold values from -6 to 6
Outputs:
- out: bfloat16 [4096, 1152], P(('dp', 'mp'))
- tokens_grad: float32 [4096, 1152], P(('dp', 'mp'))
- q_weight_grad: float32 [1152, 1024], P('dp', 'mp')
- kv_weight_grad: float32 [1152, 512], P('dp')
- o_weight_grad: float32 [1024, 1152], P('mp', 'dp')
- gate_up_weight_grad: float32 [2, 1152, 6912], P(None, 'dp', 'mp')
- down_weight_grad: float32 [6912, 1152], P('mp', 'dp')
- attn_pre_gain_grad: float32 [1152], P('dp')
- attn_post_gain_grad: float32 [1152], P('dp')
- ff_pre_gain_grad: float32 [1152], P('dp')
- ff_post_gain_grad: float32 [1152], P('dp')
- query_gain_grad: float32 [256], P('dp')
- key_gain_grad: float32 [256], P('dp')
Inputs may be any that keep to these rules, and one draw needn't show every extreme that they name: `segment_ids`: segment ids never fall; document 0 and document 2 each hold 1 to 256 tokens, document 1 the rest. Within a document, positions rise by one from token to token; document 0 starts at position 0, document 2 at 0 to 1023, and the last token of document 1 has position 5118.
All inputs are finite; a program needn't handle non-finite values.
Results may differ from a plain program's by a relative error of at most 0.028.
Values may be sent and summed in bfloat16 or wider, within the bound.
A program may use at most 128 MiB of HBM per device.

v0:
```python
from functools import partial
import jax
import jax.numpy as jnp
from jax import lax
from jax.sharding import PartitionSpec as P

WINDOW = 512
EPS = 1e-06
NEG = -1e30


def from_behind(value, axis, steps):
    count = lax.axis_size(axis)
    leading, last = (max(0, -steps), min(count, count - steps))
    return lax.ppermute(value, axis, [(source, source + steps) for source in range(leading, last)])


def shifted(value, axis, shift):
    count = lax.axis_size(axis)
    return lax.ppermute(value, axis, [(i, (i + shift) % count) for i in range(count)])


def gather_relative(value):
    count = lax.axis_size("mp")
    return [value] + [shifted(value, "mp", -step) for step in range(1, count)]


def gather_ordered(value):
    count = lax.axis_size("mp")
    rows = value.shape[0]
    me = lax.axis_index("mp")
    whole = jnp.zeros((count * rows,) + value.shape[1:], value.dtype)
    for step, block in enumerate(gather_relative(value)):
        owner = lax.rem(me + step, count)
        whole = lax.dynamic_update_slice_in_dim(whole, block, owner * rows, axis=0)
    return whole


def scatter_relative(blocks):
    total = blocks[0].astype(jnp.float32)
    for step in range(1, len(blocks)):
        total = total + shifted(blocks[step], "mp", step).astype(jnp.float32)
    return total


def scatter_ordered(value):
    count = lax.axis_size("mp")
    rows = value.shape[0] // count
    me = lax.axis_index("mp")
    return scatter_relative(
        [
            lax.dynamic_slice_in_dim(value, lax.rem(me + step, count) * rows, rows, axis=0)
            for step in range(count)
        ]
    )


def split_rows(value):
    rows = value.shape[0] // lax.axis_size("mp")
    return [value[i * rows : (i + 1) * rows] for i in range(lax.axis_size("mp"))]


def sum_over_mp(value):
    total = value.astype(jnp.float32)
    for step in range(1, lax.axis_size("mp")):
        total = total + shifted(value, "mp", step).astype(jnp.float32)
    return total


def normalize(value, gain):
    return value * lax.rsqrt(jnp.mean(value * value, axis=-1, keepdims=True) + EPS) * gain


def rotary_tables(positions, width):
    half_width = width // 2
    frequency = jnp.power(10000.0, -jnp.arange(half_width, dtype=jnp.float32) * (2.0 / width))
    angles = positions.astype(jnp.float32)[:, None] * frequency[None, :]
    return (jnp.cos(angles), jnp.sin(angles))


def rotate(value, cosine, sine):
    half_width = value.shape[-1] // 2
    first_half = value[..., :half_width]
    second_half = value[..., half_width:]
    return jnp.concatenate(
        [first_half * cosine - second_half * sine, second_half * cosine + first_half * sine],
        axis=-1,
    )


def prepare_head(pre_value, gain, cosine, sine):
    return rotate(normalize(pre_value, gain), cosine, sine)


def gated_units(gate, up_part):
    return jax.nn.gelu(gate, approximate=True) * up_part


def norm_back(value, gain, grad):
    unused, pull = jax.vjp(normalize, value, gain)
    return pull(grad)


def local(
    tokens,
    segment_ids,
    positions,
    q_weight,
    kv_weight,
    o_weight,
    gate_up_weight,
    down_weight,
    attn_pre_gain,
    attn_post_gain,
    ff_pre_gain,
    ff_post_gain,
    query_gain,
    key_gain,
    out_grad,
):
    rows = q_weight.shape[0]
    head_size = q_weight.shape[1]
    width = rows * lax.axis_size("dp")
    gain_rows = query_gain.shape[0]
    small_gains = [jnp.pad(item, (0, rows - gain_rows)) for item in (query_gain, key_gain)]
    gain_columns = jnp.stack(
        [attn_pre_gain, attn_post_gain, ff_pre_gain, ff_post_gain] + small_gains, axis=1
    )
    gain_columns = jnp.pad(gain_columns, ((0, 0), (0, 128 - gain_columns.shape[1])))
    packed = jnp.concatenate([q_weight, kv_weight, jnp.transpose(o_weight), gain_columns], axis=1)
    packed_full = lax.all_gather(packed, "dp", axis=0, tiled=True)
    gate_up_full = lax.all_gather(gate_up_weight, "dp", axis=1, tiled=True)
    down_full = lax.all_gather(down_weight, "dp", axis=1, tiled=True)
    joint_weight = packed_full[:, : 3 * head_size]
    output_turned = packed_full[:, 3 * head_size : 4 * head_size]
    gain_block = jnp.transpose(packed_full[:, 4 * head_size :]).astype(jnp.float32)
    gains = [gain_block[i] for i in range(4)] + [
        gain_block[i].reshape(-1, rows)[:, :gain_rows].reshape(-1) for i in (4, 5)
    ]
    length = segment_ids.shape[0]
    reach = -(-WINDOW // length)
    block_size = min(512, length)
    score_scale = head_size ** (-0.5)
    span = block_size + WINDOW
    cosine, sine = rotary_tables(positions, head_size)
    distance = (
        jnp.arange(block_size, dtype=jnp.int32)[:, None]
        + WINDOW
        - jnp.arange(span, dtype=jnp.int32)[None, :]
    )
    inside = (distance >= 0) & (distance < WINDOW)
    residual = tokens.astype(jnp.float32)
    attn_local = normalize(residual, gains[0]).astype(jnp.bfloat16)
    attn_in = gather_ordered(attn_local)
    projected = jnp.dot(attn_in, joint_weight, preferred_element_type=jnp.float32)
    query_pre = projected[:, :head_size]
    key_pre = projected[:, head_size : 2 * head_size]
    value_pre = projected[:, 2 * head_size :]
    queries = prepare_head(query_pre, gains[4], cosine, sine).astype(jnp.bfloat16)
    keys = prepare_head(key_pre, gains[5], cosine, sine).astype(jnp.bfloat16)
    values = value_pre.astype(jnp.bfloat16)
    marks = (segment_ids + 1).astype(jnp.bfloat16)
    key_parts, value_parts, mark_parts = ([], [], [])
    step = 1
    moved = from_behind((keys, values, marks), "dp", step)
    key_parts.append(moved[0])
    value_parts.append(moved[1])
    mark_parts.append(moved[2])
    all_keys = jnp.concatenate(key_parts + [keys], axis=0)
    all_values = jnp.concatenate(value_parts + [values], axis=0)
    all_marks = jnp.concatenate(mark_parts + [marks], axis=0)

    def block_parts(start):
        first_key = start + reach * length - WINDOW
        visible = inside & (marks[:, None] == all_marks[None, :])
        product = (
            jnp.einsum("qd,kd->qk", queries, all_keys, preferred_element_type=jnp.float32)
            * score_scale
        )
        return (first_key, queries, all_keys, all_values, jnp.where(visible, product, NEG))

    mixed_parts, total_parts = ([], [])
    start = 0
    first_key, query_block, key_block, value_block, scores = block_parts(start)
    highest = jnp.max(scores, axis=-1, keepdims=True)
    expo = jnp.exp(scores - highest)
    denominator = jnp.sum(expo, axis=-1, keepdims=True)
    probs = (expo / denominator).astype(jnp.bfloat16)
    mixed_parts.append(jnp.dot(probs, value_block, preferred_element_type=jnp.float32))
    total_parts.append(highest + jnp.log(denominator))
    attended = mixed_parts[0].astype(jnp.bfloat16)
    log_totals = total_parts[0]
    attn_out = scatter_ordered(
        jnp.einsum("le,de->ld", attended, output_turned, preferred_element_type=jnp.float32).astype(
            jnp.bfloat16
        )
    )
    middle = residual + normalize(attn_out, gains[1])
    ff_local = normalize(middle, gains[2]).astype(jnp.bfloat16)
    ff_in = jnp.concatenate(gather_relative(ff_local), axis=0)
    gate = jnp.dot(ff_in, gate_up_full[0], preferred_element_type=jnp.float32)
    up_part = jnp.dot(ff_in, gate_up_full[1], preferred_element_type=jnp.float32)
    hidden = gated_units(gate, up_part).astype(jnp.bfloat16)
    ff_out = scatter_relative(
        split_rows(
            jnp.dot(hidden, down_full, preferred_element_type=jnp.float32).astype(jnp.bfloat16)
        )
    )
    result = (middle + normalize(ff_out, gains[3])).astype(jnp.bfloat16)
    top_grad = out_grad.astype(jnp.float32)
    ff_out_grad, ff_post_grad = norm_back(ff_out, gains[3], top_grad)
    ff_grad_all = jnp.concatenate(gather_relative(ff_out_grad.astype(jnp.bfloat16)), axis=0)
    hidden_grad = jnp.einsum(
        "ld,fd->lf", ff_grad_all, down_full, preferred_element_type=jnp.float32
    )
    down_grad_turned = jnp.einsum(
        "ld,lf->df", ff_grad_all, hidden, preferred_element_type=jnp.float32
    )
    unused, unit_pull = jax.vjp(gated_units, gate, up_part)
    gate_grad, up_grad = unit_pull(hidden_grad)
    gate_low = gate_grad.astype(jnp.bfloat16)
    up_low = up_grad.astype(jnp.bfloat16)
    gate_turned = jnp.einsum("ld,lf->df", ff_in, gate_low, preferred_element_type=jnp.float32)
    up_turned = jnp.einsum("ld,lf->df", ff_in, up_low, preferred_element_type=jnp.float32)
    ff_in_partial = (
        jnp.einsum("lf,df->ld", gate_low, gate_up_full[0], preferred_element_type=jnp.float32)
        + jnp.einsum("lf,df->ld", up_low, gate_up_full[1], preferred_element_type=jnp.float32)
    ).astype(jnp.bfloat16)
    ff_in_partial, down_low, gate_turned_low, up_turned_low = lax.optimization_barrier(
        (
            ff_in_partial,
            down_grad_turned.astype(jnp.bfloat16),
            gate_turned.astype(jnp.bfloat16),
            up_turned.astype(jnp.bfloat16),
        )
    )
    feed_forward_owned = tuple(
        (
            lax.psum_scatter(item, "dp", scatter_dimension=0, tiled=True)
            for item in (down_low, gate_turned_low, up_turned_low)
        )
    )
    ff_in_grad = scatter_relative(split_rows(ff_in_partial))
    middle_part, ff_pre_grad = norm_back(middle, gains[2], ff_in_grad)
    middle_grad = top_grad + middle_part
    attn_out_grad, attn_post_grad = norm_back(attn_out, gains[1], middle_grad)
    attn_grad_all = gather_ordered(attn_out_grad.astype(jnp.bfloat16))
    attended_grad = jnp.einsum(
        "ld,de->le", attn_grad_all, output_turned, preferred_element_type=jnp.float32
    ).astype(jnp.bfloat16)
    output_grad_turned = jnp.einsum(
        "ld,le->de", attn_grad_all, attended, preferred_element_type=jnp.float32
    )
    key_grad_all = jnp.zeros(((reach + 1) * length, head_size), jnp.float32)
    value_grad_all = jnp.zeros(((reach + 1) * length, head_size), jnp.float32)
    start = 0
    first_key, query_block, key_block, value_block, scores = block_parts(start)
    probs = jnp.exp(scores - log_totals)
    probs_low = probs.astype(jnp.bfloat16)
    value_grad_all = value_grad_all.at[first_key : first_key + span].add(
        jnp.einsum("qk,qd->kd", probs_low, attended_grad, preferred_element_type=jnp.float32)
    )
    prob_grad = jnp.einsum(
        "qd,kd->qk", attended_grad, value_block, preferred_element_type=jnp.float32
    )
    inner = jnp.sum(probs * prob_grad, axis=-1, keepdims=True)
    score_grad = (probs * (prob_grad - inner)).astype(jnp.bfloat16)
    query_parts = jnp.dot(score_grad, key_block, preferred_element_type=jnp.float32) * score_scale
    key_grad_all = key_grad_all.at[first_key : first_key + span].add(
        jnp.einsum("qk,qd->kd", score_grad, query_block, preferred_element_type=jnp.float32)
        * score_scale
    )
    own_keys = key_grad_all[reach * length :]
    own_values = value_grad_all[reach * length :]
    step = 1
    slot = reach - step
    returned = (
        from_behind(
            key_grad_all[slot * length : (slot + 1) * length].astype(jnp.bfloat16), "dp", -step
        ).astype(jnp.float32),
        from_behind(
            value_grad_all[slot * length : (slot + 1) * length].astype(jnp.bfloat16), "dp", -step
        ).astype(jnp.float32),
    )
    own_keys = own_keys + returned[0]
    own_values = own_values + returned[1]
    unused, query_pull = jax.vjp(
        partial(prepare_head, cosine=cosine, sine=sine), query_pre, gains[4]
    )
    query_pre_grad, query_gain_grad = query_pull(query_parts)
    unused, key_pull = jax.vjp(partial(prepare_head, cosine=cosine, sine=sine), key_pre, gains[5])
    key_pre_grad, key_gain_grad = key_pull(own_keys)
    joint_grad_rows = jnp.concatenate([query_pre_grad, key_pre_grad, own_values], axis=1).astype(
        jnp.bfloat16
    )
    joint_grad = jnp.einsum(
        "ld,lc->dc", attn_in, joint_grad_rows, preferred_element_type=jnp.float32
    )
    attn_in_grad = scatter_ordered(
        jnp.einsum(
            "lc,dc->ld", joint_grad_rows, joint_weight, preferred_element_type=jnp.float32
        ).astype(jnp.bfloat16)
    )
    tokens_part, attn_pre_grad = norm_back(residual, gains[0], attn_in_grad)
    tokens_grad = middle_grad + tokens_part
    small_grads = [
        jnp.pad(item.reshape(-1, gain_rows), ((0, 0), (0, rows - gain_rows))).reshape(-1)
        for item in (query_gain_grad, key_gain_grad)
    ]
    gain_grads = jnp.stack(
        [attn_pre_grad, attn_post_grad, ff_pre_grad, ff_post_grad] + small_grads, axis=1
    )
    gain_grads = jnp.pad(gain_grads, ((0, 0), (0, 128 - gain_grads.shape[1])))
    packed_grad = jnp.concatenate(
        [
            joint_grad[:, :head_size].astype(jnp.bfloat16),
            output_grad_turned.astype(jnp.bfloat16),
            joint_grad[:, head_size:].astype(jnp.bfloat16),
            gain_grads.astype(jnp.bfloat16),
        ],
        axis=1,
    )
    packed_grad, feed_forward_owned = lax.optimization_barrier((packed_grad, feed_forward_owned))
    down_owned = jnp.transpose(feed_forward_owned[0]).astype(jnp.float32)
    gate_up_owned = jnp.stack(feed_forward_owned[1:], axis=0).astype(jnp.float32)
    packed_owned = lax.psum_scatter(packed_grad, "dp", scatter_dimension=0, tiled=True)
    query_owned = packed_owned[:, :head_size].astype(jnp.float32)
    output_owned = jnp.transpose(packed_owned[:, head_size : 2 * head_size]).astype(jnp.float32)
    summed = sum_over_mp(packed_owned[:, 2 * head_size :])
    keyval_owned = summed[:, : 2 * head_size]
    gain_owned = jnp.transpose(summed[:, 2 * head_size :])
    return (
        result,
        tokens_grad,
        query_owned,
        keyval_owned,
        output_owned,
        gate_up_owned,
        down_owned,
        gain_owned[0],
        gain_owned[1],
        gain_owned[2],
        gain_owned[3],
        gain_owned[4, :gain_rows],
        gain_owned[5, :gain_rows],
    )


def solution(mesh):
    placed = (
        P(("dp", "mp"), None),
        P("dp"),
        P("dp"),
        P("dp", "mp"),
        P("dp", None),
        P("mp", "dp"),
        P(None, "dp", "mp"),
        P("mp", "dp"),
        P("dp"),
        P("dp"),
        P("dp"),
        P("dp"),
        P("dp"),
        P("dp"),
        P(("dp", "mp"), None),
    )
    return jax.shard_map(
        local,
        mesh=mesh,
        in_specs=placed,
        out_specs=(
            P(("dp", "mp"), None),
            P(("dp", "mp"), None),
            P("dp", "mp"),
            P("dp", None),
            P("mp", "dp"),
            P(None, "dp", "mp"),
            P("mp", "dp"),
            P("dp"),
            P("dp"),
            P("dp"),
            P("dp"),
            P("dp"),
            P("dp"),
        ),
        check_vma=False,
    )
```

profile of v0, /device:TPU:0, one launch (start us, length us, event | category | flops | bytes accessed | tf_op | source)
XLA Modules:
  0.0 732.3 jit_solution(13621012869615528322)
XLA Ops:
  14.2 56.9 %all-gather.4.cloned.1.call-done = bf16[1152,1152]{1,0:T(8,128)(2,1)} async-done(((bf16[144,1152]{1,0:T(8,128)(2,1)}), bf16[1152,1152]{1,0:T(8,128)(2,1)}) %all-gather.4.cloned.1.call-update) | async-done | bytes 2654224 | tf_op jit(solution)/shard_map/all_gather | solution.py:131
  80.4 9.1 %collective-permute-done.2 = bf16[128,1152]{1,0:T(8,128)(2,1)S(1)} collective-permute-done((bf16[128,1152]{1,0:T(8,128)(2,1)S(1)}, bf16[128,1152]{1,0:T(8,128)(2,1)S(1)}, u32[]{:S(2)}, u32[]{:S(2)}) %collective-permute-start.2) | collective-permute-done | bytes 294944 | tf_op jit(solution)/shard_map/ppermute | solution.py:20
  103.1 10.1 %collective-permute-start.5 = (bf16[512,256]{1,0:T(8,128)(2,1)S(1)}, bf16[512,256]{1,0:T(8,128)(2,1)S(1)}, u32[]{:S(2)}, u32[]{:S(2)}) collective-permute-start(bf16[512,256]{1,0:T(8,128)(2,1)S(1)} %slice.321), channel_id=1, source_target_pairs={{0,4},{4,8},{8,12},{12,16},{16,20},{20,24},{24,28},{1,5},{5,9},{9,... | collective-permute-start | bytes 786440 | tf_op jit(solution)/shard_map/ppermute | solution.py:15
  120.8 5.7 collective-permute-done.8
  126.5 7.6 %collective-permute-done.7 = bf16[128,1152]{1,0:T(8,128)(2,1)S(1)} collective-permute-done((bf16[128,1152]{1,0:T(8,128)(2,1)S(1)}, bf16[128,1152]{1,0:T(8,128)(2,1)S(1)}, u32[]{:S(2)}, u32[]{:S(2)}) %collective-permute-start.7) | collective-permute-done | bytes 294944 | tf_op jit(solution)/shard_map/ppermute | solution.py:20
  138.2 6.0 collective-permute-done.11
  149.7 54.7 %all-gather.6.cloned.1.call-done = bf16[2,1152,1728]{2,1,0:T(8,128)(2,1)} async-done(((bf16[2,144,1728]{2,1,0:T(8,128)(2,1)}), bf16[2,1152,1728]{2,1,0:T(8,128)(2,1)}) %all-gather.6.cloned.1.call-update) | async-done | bytes 7962640 | tf_op jit(solution)/shard_map/all_gather | solution.py:132
  211.4 6.8 multiply_convert_fusion.1
  218.2 59.2 %all-gather.8.cloned.1.call-done = bf16[1728,1152]{0,1:T(8,128)(2,1)} async-done(((bf16[1728,144]{0,1:T(8,128)(2,1)}), bf16[1728,1152]{0,1:T(8,128)(2,1)}) %all-gather.8.cloned.1.call-update) | async-done | bytes 3981328 | tf_op jit(solution)/shard_map/all_gather | solution.py:133
  277.4 5.3 convolution_convert_fusion.5
  289.2 9.2 %collective-permute-done.13 = bf16[128,1152]{1,0:T(8,128)(2,1)S(1)} collective-permute-done((bf16[128,1152]{1,0:T(8,128)(2,1)S(1)}, bf16[128,1152]{1,0:T(8,128)(2,1)S(1)}, u32[]{:S(2)}, u32[]{:S(2)}) %collective-permute-start.13) | collective-permute-done | bytes 294944 | tf_op jit(solution)/shard_map/ppermute | solution.py:20
  302.6 6.7 collective-permute-done.17
  318.6 8.4 %multiply_convert_fusion = (bf16[512,1728]{0,1:T(8,128)(2,1)S(1)}, bf16[512,1728]{0,1:T(8,128)(2,1)S(1)}) fusion(f32[512,1728]{0,1:T(8,128)S(1)} %copy-done.77, f32[512,1728]{0,1:T(8,128)} %get-tuple-element.185, bf16[1728,1152]{0,1:T(8,128)(2,1)S(1)} %copy-done.67, bf16[128,1152]{1,0:T(8,128)(2,1)S(1)} %collective-permute-done.17, ...), kind=kOutput, calls=%fused_computation.20 | convolution fusion | flops 2064384000 | bytes 15777792 | tf_op jit(solution)/shard_map/ld,fd->lf/dot_general | solution.py:213
  329.7 5.4 convolution_convert_fusion.1
  344.1 6.5 copy.60
  350.7 6.5 copy.62
  362.7 6.5 copy.64
  369.2 7.4 %collective-permute-done.19 = bf16[128,1152]{1,0:T(8,128)(2,1)} collective-permute-done((bf16[128,1152]{1,0:T(8,128)(2,1)}, bf16[128,1152]{1,0:T(8,128)(2,1)}, u32[]{:S(2)}, u32[]{:S(2)}) %collective-permute-start.19) | collective-permute-done | bytes 294944 | tf_op jit(solution)/shard_map/ppermute | solution.py:20
  388.4 6.6 collective-permute-done.22
  403.9 13.7 %collective-permute-done.24 = bf16[512,256]{1,0:T(8,128)(2,1)S(1)} collective-permute-done((bf16[512,256]{1,0:T(8,128)(2,1)S(1)}, bf16[512,256]{1,0:T(8,128)(2,1)S(1)}, u32[]{:S(2)}, u32[]{:S(2)}) %collective-permute-start.24) | collective-permute-done | bytes 262176 | tf_op jit(solution)/shard_map/ppermute | solution.py:15
  449.0 89.0 %reduce-scatter.15.cloned.1.call-done = bf16[144,1728]{1,0:T(8,128)(2,1)} async-done(((bf16[1152,1728]{1,0:T(8,128)(2,1)}), bf16[144,1728]{1,0:T(8,128)(2,1)}) %reduce-scatter.15.cloned.1.call-update) | async-done | bytes 497680
  540.2 88.7 %reduce-scatter.17.cloned.1.call-done = bf16[144,1728]{1,0:T(8,128)(2,1)} async-done(((bf16[1152,1728]{1,0:T(8,128)(2,1)}), bf16[144,1728]{1,0:T(8,128)(2,1)}) %reduce-scatter.17.cloned.1.call-update) | async-done | bytes 497680
  642.2 62.7 %reduce-scatter.19.cloned.1.call-done = bf16[144,1152]{1,0:T(8,128)(2,1)} async-done(((bf16[1152,1152]{1,0:T(8,128)(2,1)}), bf16[144,1152]{1,0:T(8,128)(2,1)}) %reduce-scatter.19.cloned.1.call-update) | async-done | bytes 331792
  713.1 9.9 %collective-permute-done.30 = bf16[144,640]{0,1:T(8,128)(2,1)S(1)} collective-permute-done((bf16[144,640]{0,1:T(8,128)(2,1)S(1)}, bf16[144,640]{0,1:T(8,128)(2,1)S(1)}, u32[]{:S(2)}, u32[]{:S(2)}) %collective-permute-start.30) | collective-permute-done | bytes 184352 | tf_op jit(solution)/shard_map/ppermute | solution.py:20
  (360 shorter events, 168.2 us)
Async XLA Ops:
  7.2 63.9 %all-gather.4.cloned.1.call-start = ((), (), s32[]{:S(2)}) async-start(), calls=%async_computation.4 | async-start | bytes 2985984 | tf_op jit(solution)/shard_map/all_gather | solution.py:131
  13.2 191.2 %all-gather.6.cloned.1.call-start = ((), (), s32[]{:S(2)}) async-start(), calls=%async_computation.5 | async-start | bytes 9289728 | tf_op jit(solution)/shard_map/all_gather | solution.py:132
  13.9 263.5 %all-gather.8.cloned.1.call-start = ((), (), s32[]{:S(2)}) async-start(), calls=%async_computation.6 | async-start | bytes 4644864 | tf_op jit(solution)/shard_map/all_gather | solution.py:133
  74.2 372.5 %reduce-scatter.13.cloned.1.call-start = ((), (), s32[]{:S(2)}) async-start(), calls=%async_computation.7 | async-start | bytes 4644864
  74.5 15.0 %collective-permute-start.2 = (bf16[128,1152]{1,0:T(8,128)(2,1)S(1)}, bf16[128,1152]{1,0:T(8,128)(2,1)S(1)}, u32[]{:S(2)}, u32[]{:S(2)}) collective-permute-start(bf16[128,1152]{1,0:T(8,128)(2,1)S(1)} %get-tuple-element.141), channel_id=1, source_target_pairs={{0,2},{1,3},{2,0},{3,1},{4,6},{5,7},{6,4},{7,5},{8,10},{9,11},{10,... | collective-permute-start | bytes 884744 | tf_op jit(solution)/shard_map/ppermute | solution.py:20
  76.0 13.8 %collective-permute-start.3 = (bf16[128,1152]{1,0:T(8,128)(2,1)S(1)}, bf16[128,1152]{1,0:T(8,128)(2,1)S(1)}, u32[]{:S(2)}, u32[]{:S(2)}) collective-permute-start(bf16[128,1152]{1,0:T(8,128)(2,1)S(1)} %get-tuple-element.141), channel_id=1, source_target_pairs={{0,1},{1,2},{2,3},{3,0},{4,5},{5,6},{6,7},{7,4},{8,9},{9,10},{10,1... | collective-permute-start | bytes 884744 | tf_op jit(solution)/shard_map/ppermute | solution.py:20
  94.9 18.2 %collective-permute-start.4 = (bf16[512,256]{1,0:T(8,128)(2,1)S(1)}, bf16[512,256]{1,0:T(8,128)(2,1)S(1)}, u32[]{:S(2)}, u32[]{:S(2)}) collective-permute-start(bf16[512,256]{1,0:T(8,128)(2,1)S(1)} %pad_maximum_fusion.9), channel_id=1, source_target_pairs={{0,4},{4,8},{8,12},{12,16},{16,20},{20,24},{24,28},{1,5},{5,9},{9,... | collective-permute-start | bytes 786440 | tf_op jit(solution)/shard_map/ppermute | solution.py:15
  103.1 13.9 %collective-permute-start.5 = (bf16[512,256]{1,0:T(8,128)(2,1)S(1)}, bf16[512,256]{1,0:T(8,128)(2,1)S(1)}, u32[]{:S(2)}, u32[]{:S(2)}) collective-permute-start(bf16[512,256]{1,0:T(8,128)(2,1)S(1)} %slice.321), channel_id=1, source_target_pairs={{0,4},{4,8},{8,12},{12,16},{16,20},{20,24},{24,28},{1,5},{5,9},{9,... | collective-permute-start | bytes 786440 | tf_op jit(solution)/shard_map/ppermute | solution.py:15
  119.6 14.6 %collective-permute-start.7 = (bf16[128,1152]{1,0:T(8,128)(2,1)S(1)}, bf16[128,1152]{1,0:T(8,128)(2,1)S(1)}, u32[]{:S(2)}, u32[]{:S(2)}) collective-permute-start(bf16[128,1152]{1,0:T(8,128)(2,1)S(1)} %get-tuple-element.159), channel_id=1, source_target_pairs={{0,2},{1,3},{2,0},{3,1},{4,6},{5,7},{6,4},{7,5},{8,10},{9,11},{10,... | collective-permute-start | bytes 884744 | tf_op jit(solution)/shard_map/ppermute | solution.py:20
  120.6 14.1 %collective-permute-start.6 = (bf16[128,1152]{1,0:T(8,128)(2,1)S(1)}, bf16[128,1152]{1,0:T(8,128)(2,1)S(1)}, u32[]{:S(2)}, u32[]{:S(2)}) collective-permute-start(bf16[128,1152]{1,0:T(8,128)(2,1)S(1)} %get-tuple-element.157), channel_id=1, source_target_pairs={{0,1},{1,2},{2,3},{3,0},{4,5},{5,6},{6,7},{7,4},{8,9},{9,10},{10,1... | collective-permute-start | bytes 884744 | tf_op jit(solution)/shard_map/ppermute | solution.py:20
  282.9 15.5 %collective-permute-start.13 = (bf16[128,1152]{1,0:T(8,128)(2,1)S(1)}, bf16[128,1152]{1,0:T(8,128)(2,1)S(1)}, u32[]{:S(2)}, u32[]{:S(2)}) collective-permute-start(bf16[128,1152]{1,0:T(8,128)(2,1)S(1)} %get-tuple-element.156), channel_id=1, source_target_pairs={{0,2},{1,3},{2,0},{3,1},{4,6},{5,7},{6,4},{7,5},{8,10},{9,11},{10,... | collective-permute-start | bytes 884744 | tf_op jit(solution)/shard_map/ppermute | solution.py:20
  284.4 14.1 %collective-permute-start.12 = (bf16[128,1152]{1,0:T(8,128)(2,1)S(1)}, bf16[128,1152]{1,0:T(8,128)(2,1)S(1)}, u32[]{:S(2)}, u32[]{:S(2)}) collective-permute-start(bf16[128,1152]{1,0:T(8,128)(2,1)S(1)} %get-tuple-element.154), channel_id=1, source_target_pairs={{0,1},{1,2},{2,3},{3,0},{4,5},{5,6},{6,7},{7,4},{8,9},{9,10},{10,1... | collective-permute-start | bytes 884744 | tf_op jit(solution)/shard_map/ppermute | solution.py:20
  350.6 187.4 %reduce-scatter.15.cloned.1.call-start = ((), (), s32[]{:S(2)}) async-start(), calls=%async_computation.8 | async-start | bytes 4644864
  357.2 271.7 %reduce-scatter.17.cloned.1.call-start = ((), (), s32[]{:S(2)}) async-start(), calls=%async_computation.9 | async-start | bytes 4644864
  361.2 15.4 %collective-permute-start.19 = (bf16[128,1152]{1,0:T(8,128)(2,1)}, bf16[128,1152]{1,0:T(8,128)(2,1)}, u32[]{:S(2)}, u32[]{:S(2)}) collective-permute-start(bf16[128,1152]{1,0:T(8,128)(2,1)} %get-tuple-element.153), channel_id=1, source_target_pairs={{0,2},{1,3},{2,0},{3,1},{4,6},{5,7},{6,4},{7,5},{8,10},{9,11},{10,... | collective-permute-start | bytes 884744 | tf_op jit(solution)/shard_map/ppermute | solution.py:20
  362.7 14.0 %collective-permute-start.18 = (bf16[128,1152]{1,0:T(8,128)(2,1)}, bf16[128,1152]{1,0:T(8,128)(2,1)}, u32[]{:S(2)}, u32[]{:S(2)}) collective-permute-start(bf16[128,1152]{1,0:T(8,128)(2,1)} %get-tuple-element.151), channel_id=1, source_target_pairs={{0,1},{1,2},{2,3},{3,0},{4,5},{5,6},{6,7},{7,4},{8,9},{9,10},{10,1... | collective-permute-start | bytes 884744 | tf_op jit(solution)/shard_map/ppermute | solution.py:20
  369.2 335.7 %reduce-scatter.19.cloned.1.call-start = ((), (), s32[]{:S(2)}) async-start(), calls=%async_computation.10 | async-start | bytes 2985984
  381.2 13.8 %collective-permute-start.22 = (bf16[128,1152]{1,0:T(8,128)(2,1)S(1)}, bf16[128,1152]{1,0:T(8,128)(2,1)S(1)}, u32[]{:S(2)}, u32[]{:S(2)}) collective-permute-start(bf16[128,1152]{1,0:T(8,128)(2,1)S(1)} %get-tuple-element.132), channel_id=1, source_target_pairs={{0,2},{1,3},{2,0},{3,1},{4,6},{5,7},{6,4},{7,5},{8,10},{9,11},{10,... | collective-permute-start | bytes 884744 | tf_op jit(solution)/shard_map/ppermute | solution.py:20
  381.9 14.1 %collective-permute-start.23 = (bf16[128,1152]{1,0:T(8,128)(2,1)S(1)}, bf16[128,1152]{1,0:T(8,128)(2,1)S(1)}, u32[]{:S(2)}, u32[]{:S(2)}) collective-permute-start(bf16[128,1152]{1,0:T(8,128)(2,1)S(1)} %get-tuple-element.132), channel_id=1, source_target_pairs={{0,1},{1,2},{2,3},{3,0},{4,5},{5,6},{6,7},{7,4},{8,9},{9,10},{10,1... | collective-permute-start | bytes 884744 | tf_op jit(solution)/shard_map/ppermute | solution.py:20
  397.2 22.6 %collective-permute-start.25 = (bf16[512,256]{1,0:T(8,128)(2,1)S(1)}, bf16[512,256]{1,0:T(8,128)(2,1)S(1)}, u32[]{:S(2)}, u32[]{:S(2)}) collective-permute-start(bf16[512,256]{1,0:T(8,128)(2,1)S(1)} %slice.319), channel_id=1, source_target_pairs={{4,0},{8,4},{12,8},{16,12},{20,16},{24,20},{28,24},{5,1},{9,5},{13... | collective-permute-start | bytes 786440 | tf_op jit(solution)/shard_map/ppermute | solution.py:15
  400.6 16.9 %collective-permute-start.24 = (bf16[512,256]{1,0:T(8,128)(2,1)S(1)}, bf16[512,256]{1,0:T(8,128)(2,1)S(1)}, u32[]{:S(2)}, u32[]{:S(2)}) collective-permute-start(bf16[512,256]{1,0:T(8,128)(2,1)S(1)} %slice.320), channel_id=1, source_target_pairs={{4,0},{8,4},{12,8},{16,12},{20,16},{24,20},{28,24},{5,1},{9,5},{13... | collective-permute-start | bytes 786440 | tf_op jit(solution)/shard_map/ppermute | solution.py:15
  422.3 14.2 %collective-permute-start.26 = (bf16[128,1152]{1,0:T(8,128)(2,1)S(1)}, bf16[128,1152]{1,0:T(8,128)(2,1)}, u32[]{:S(2)}, u32[]{:S(2)}) collective-permute-start(bf16[128,1152]{1,0:T(8,128)(2,1)S(1)} %get-tuple-element.148), channel_id=1, source_target_pairs={{0,1},{1,2},{2,3},{3,0},{4,5},{5,6},{6,7},{7,4},{8,9},{9,10},{10,1... | collective-permute-start | bytes 884744 | tf_op jit(solution)/shard_map/ppermute | solution.py:20
  706.1 16.9 %collective-permute-start.30 = (bf16[144,640]{0,1:T(8,128)(2,1)S(1)}, bf16[144,640]{0,1:T(8,128)(2,1)S(1)}, u32[]{:S(2)}, u32[]{:S(2)}) collective-permute-start(bf16[144,640]{0,1:T(8,128)(2,1)S(1)} %copy.69), channel_id=1, source_target_pairs={{0,2},{1,3},{2,0},{3,1},{4,6},{5,7},{6,4},{7,5},{8,10},{9,11},{10,... | collective-permute-start | bytes 552968 | tf_op jit(solution)/shard_map/ppermute | solution.py:20
  707.6 15.5 %collective-permute-start.29 = (bf16[144,640]{0,1:T(8,128)(2,1)S(1)}, bf16[144,640]{0,1:T(8,128)(2,1)S(1)}, u32[]{:S(2)}, u32[]{:S(2)}) collective-permute-start(bf16[144,640]{0,1:T(8,128)(2,1)S(1)} %copy.69), channel_id=1, source_target_pairs={{0,1},{1,2},{2,3},{3,0},{4,5},{5,6},{6,7},{7,4},{8,9},{9,10},{10,1... | collective-permute-start | bytes 552968 | tf_op jit(solution)/shard_map/ppermute | solution.py:20
  (97 other events, 906.3 us)
Sparse Core Ops, SparseCore 0:
  13.3 57.7 all-gather.3
  73.3 131.1 all-gather.5
  206.6 70.7 all-gather.7
  350.7 95.9 reduce-scatter.12
  450.5 87.4 reduce-scatter.14
  541.4 87.4 reduce-scatter.16
  634.6 70.2 reduce-scatter.18
where the time goes:
time: 740 us; the launch traced here: 732 us
  waiting for transfers between devices  533 us (72%)
  local copies, waits for them, and re-layouts  65.2 us (9%)
  matrix products  59.8 us (8%)
  starting transfers between devices  36.2 us (5%)
  other arithmetic  22.5 us (3%)
  between operations  15.8 us (2%)
    unnamed x11, waiting for transfers between devices  246 us
    ppermute x27, waiting for transfers between devices, shifted(): lax.ppermute(value, axis, [(i, (i + shift) % count) for i in range(count)])  99.2 us
    all_gather x1, waiting for transfers between devices, local(): down_full = lax.all_gather(down_weight, 'dp', axis=1, tiled=True)  59.2 us
    all_gather x1, waiting for transfers between devices, local(): packed_full = lax.all_gather(packed, 'dp', axis=0, tiled=True)  56.9 us
    all_gather x1, waiting for transfers between devices, local(): gate_up_full = lax.all_gather(gate_up_weight, 'dp', axis=1, tiled=True)  54.7 us
    unnamed x175, local copies, waits for them, and re-layouts  34.6 us
    ppermute x5, starting transfers between devices, from_behind(): lax.ppermute(value, axis, [(source, source + steps) for source in range(l...  19.4 us
    ppermute x5, waiting for transfers between devices, from_behind(): lax.ppermute(value, axis, [(source, source + steps) for source in range(l...  17.3 us
  transfers between devices with their start and end apart: 39, of which 34 were waited for; matrix products, arithmetic and copies ran while one was open for 11% of the time, Pallas kernels for 0%

commit v1 on v0

--- a/solution.py
+++ b/solution.py
@@ -128,7 +128,16 @@
     )
     gain_columns = jnp.pad(gain_columns, ((0, 0), (0, 128 - gain_columns.shape[1])))
     packed = jnp.concatenate([q_weight, kv_weight, jnp.transpose(o_weight), gain_columns], axis=1)
-    packed_full = lax.all_gather(packed, "dp", axis=0, tiled=True)
+    shard = packed
+    ways, here, step_2 = (lax.axis_size("dp"), lax.axis_index("dp"), shard.shape[0])
+    shape = [n * ways if d == 0 else n for d, n in enumerate(shard.shape)]
+    full = lax.dynamic_update_slice_in_dim(
+        jnp.zeros(shape, shard.dtype), shard, here * step_2, axis=0
+    )
+    for far in range(1, ways):
+        shard = lax.ppermute(shard, "dp", [(d, (d + 1) % ways) for d in range(ways)])
+        full = lax.dynamic_update_slice_in_dim(full, shard, (here - far) % ways * step_2, axis=0)
+    packed_full = full
     gate_up_full = lax.all_gather(gate_up_weight, "dp", axis=1, tiled=True)
     down_full = lax.all_gather(down_weight, "dp", axis=1, tiled=True)
     joint_weight = packed_full[:, : 3 * head_size]

time: 740 us -> 773 us (1.045)
  waiting for transfers between devices: 533 us -> 446 us
  local copies, waits for them, and re-layouts: 65.2 us -> 151 us
  starting transfers between devices: 36.2 us -> 69 us
    ppermute x0 -> x7, waiting for transfers between devices: none -> 93.3 us  [local(): lax.ppermute(shard, 'dp', [(d, (d + 1) % ways) for d in range(ways)])]
    dynamic_update_slice x0 -> x8, local copies, waits for them, and re-layouts: none -> 65 us  [the longest x7 57.9 us: local(): lax.dynamic_update_slice_in_dim(full, shard, (here - far) % ways * step_2...]
    all_gather x1, waiting for transfers between devices: 59.2 us -> 0.01 us  [local(): down_full = lax.all_gather(down_weight, 'dp', axis=1, tiled=True)]
    all_gather x1 -> x0, waiting for transfers between devices: 56.9 us -> none  [local(): packed_full = lax.all_gather(packed, 'dp', axis=0, tiled=True)]
    all_gather x1, waiting for transfers between devices: 54.7 us -> 0.01 us  [local(): gate_up_full = lax.all_gather(gate_up_weight, 'dp', axis=1, tiled=True)]
    ppermute x27, waiting for transfers between devices: 99.2 us -> 80.7 us  [shifted(): lax.ppermute(value, axis, [(i, (i + shift) % count) for i in range(count)])]
    ppermute x27, starting transfers between devices: 16.5 us -> 34.9 us  [shifted(): lax.ppermute(value, axis, [(i, (i + shift) % count) for i in range(count)])]
    ppermute x5, starting transfers between devices: 19.4 us -> 29.8 us  [from_behind(): lax.ppermute(value, axis, [(source, source + steps) for source in range(l...]
  transfers between devices with their start and end apart: 39 -> 45, of which waited for: 34 -> 30; matrix products, arithmetic and copies ran while one was open for 11% -> 23% of each run, Pallas kernels for 0% -> 0%
where the time goes in v1:
time: 773 us; the launch traced here: 764 us
  waiting for transfers between devices  446 us (58%)
  local copies, waits for them, and re-layouts  151 us (20%)
  starting transfers between devices  69 us (9%)
  matrix products  58.8 us (8%)
  other arithmetic  23.8 us (3%)
  between operations  16.2 us (2%)
    unnamed x10, waiting for transfers between devices  247 us
    ppermute x7, waiting for transfers between devices, local(): lax.ppermute(shard, 'dp', [(d, (d + 1) % ways) for d in range(ways)])  93.3 us
    ppermute x27, waiting for transfers between devices, shifted(): lax.ppermute(value, axis, [(i, (i + shift) % count) for i in range(count)])  80.7 us
    dynamic_update_slice x7, local copies, waits for them, and re-layouts, local(): lax.dynamic_update_slice_in_dim(full, shard, (here - far) % ways * step_2...  57.9 us
    unnamed x183, local copies, waits for them, and re-layouts  37.4 us
    ppermute x27, starting transfers between devices, shifted(): lax.ppermute(value, axis, [(i, (i + shift) % count) for i in range(count)])  34.9 us
    ppermute x5, starting transfers between devices, from_behind(): lax.ppermute(value, axis, [(source, source + steps) for source in range(l...  29.8 us
    ppermute x5, waiting for transfers between devices, from_behind(): lax.ppermute(value, axis, [(source, source + steps) for source in range(l...  24.5 us
  transfers between devices with their start and end apart: 45, of which 30 were waited for; matrix products, arithmetic and copies ran while one was open for 23% of the time, Pallas kernels for 0%

profile of v1, /device:TPU:0, one launch (start us, length us, event | category | flops | bytes accessed | tf_op | source)
XLA Modules:
  0.0 764.2 jit_solution(11244543413256169150)
XLA Ops:
  16.1 11.0 %collective-permute-done.1 = bf16[144,1152]{1,0:T(8,128)(2,1)S(1)} collective-permute-done((bf16[144,1152]{1,0:T(8,128)(2,1)S(1)}, bf16[144,1152]{1,0:T(8,128)(2,1)S(1)}, u32[]{:S(2)}, u32[]{:S(2)}) %collective-permute-start.1) | collective-permute-done | bytes 331808 | tf_op jit(solution)/shard_map/ppermute | solution.py:138
  28.1 18.9 %collective-permute-done.2 = bf16[144,1152]{1,0:T(8,128)(2,1)S(1)} collective-permute-done((bf16[144,1152]{1,0:T(8,128)(2,1)S(1)}, bf16[144,1152]{1,0:T(8,128)(2,1)S(1)}, u32[]{:S(2)}, u32[]{:S(2)}) %collective-permute-start.2) | collective-permute-done | bytes 331808 | tf_op jit(solution)/shard_map/ppermute | solution.py:138
  47.0 19.5 %collective-permute-done.3 = bf16[144,1152]{1,0:T(8,128)(2,1)S(1)} collective-permute-done((bf16[144,1152]{1,0:T(8,128)(2,1)S(1)}, bf16[144,1152]{1,0:T(8,128)(2,1)S(1)}, u32[]{:S(2)}, u32[]{:S(2)}) %collective-permute-start.3) | collective-permute-done | bytes 331808 | tf_op jit(solution)/shard_map/ppermute | solution.py:138
  66.5 15.3 %collective-permute-done.4 = bf16[144,1152]{1,0:T(8,128)(2,1)S(1)} collective-permute-done((bf16[144,1152]{1,0:T(8,128)(2,1)S(1)}, bf16[144,1152]{1,0:T(8,128)(2,1)S(1)}, u32[]{:S(2)}, u32[]{:S(2)}) %collective-permute-start.4) | collective-permute-done | bytes 331808 | tf_op jit(solution)/shard_map/ppermute | solution.py:138
  81.8 17.5 %collective-permute-done.5 = bf16[144,1152]{1,0:T(8,128)(2,1)} collective-permute-done((bf16[144,1152]{1,0:T(8,128)(2,1)S(1)}, bf16[144,1152]{1,0:T(8,128)(2,1)}, u32[]{:S(2)}, u32[]{:S(2)}) %collective-permute-start.5) | collective-permute-done | bytes 331808 | tf_op jit(solution)/shard_map/ppermute | solution.py:138
  107.1 11.1 %collective-permute-done.6 = bf16[144,1152]{1,0:T(8,128)(2,1)} collective-permute-done((bf16[144,1152]{1,0:T(8,128)(2,1)}, bf16[144,1152]{1,0:T(8,128)(2,1)}, u32[]{:S(2)}, u32[]{:S(2)}) %collective-permute-start.6) | collective-permute-done | bytes 331808 | tf_op jit(solution)/shard_map/ppermute | solution.py:138
  128.6 7.1 dynamic_update_slice.50
  136.9 8.8 %dynamic_update_slice.51 = bf16[1152,1152]{0,1:T(8,128)(2,1)S(1)} dynamic-update-slice(bf16[1152,1152]{0,1:T(8,128)(2,1)S(1)} %dynamic_update_slice.50, bf16[144,1152]{0,1:T(8,128)(2,1)S(1)} %copy.59, s32[]{:T(128)S(6)} %select_n.90, s32[]{:T(128)} %constant.180.clone.1) | dynamic-update-slice | bytes 663556 | tf_op jit(solution)/shard_map/dynamic_update_slice | solution.py:139
  146.9 8.8 %dynamic_update_slice.52 = bf16[1152,1152]{0,1:T(8,128)(2,1)S(1)} dynamic-update-slice(bf16[1152,1152]{0,1:T(8,128)(2,1)S(1)} %dynamic_update_slice.51, bf16[144,1152]{0,1:T(8,128)(2,1)S(1)} %copy.60, s32[]{:T(128)S(6)} %select_n.92, s32[]{:T(128)} %constant.180.clone.1) | dynamic-update-slice | bytes 663556 | tf_op jit(solution)/shard_map/dynamic_update_slice | solution.py:139
  157.0 8.8 %dynamic_update_slice.53 = bf16[1152,1152]{0,1:T(8,128)(2,1)S(1)} dynamic-update-slice(bf16[1152,1152]{0,1:T(8,128)(2,1)S(1)} %dynamic_update_slice.52, bf16[144,1152]{0,1:T(8,128)(2,1)S(1)} %copy.61, s32[]{:T(128)S(6)} %select_n.94, s32[]{:T(128)} %constant.180.clone.1) | dynamic-update-slice | bytes 663556 | tf_op jit(solution)/shard_map/dynamic_update_slice | solution.py:139
  167.0 8.8 %dynamic_update_slice.54 = bf16[1152,1152]{0,1:T(8,128)(2,1)S(1)} dynamic-update-slice(bf16[1152,1152]{0,1:T(8,128)(2,1)S(1)} %dynamic_update_slice.53, bf16[144,1152]{0,1:T(8,128)(2,1)S(1)} %copy.62, s32[]{:T(128)S(6)} %select_n.96, s32[]{:T(128)} %constant.180.clone.1) | dynamic-update-slice | bytes 663556 | tf_op jit(solution)/shard_map/dynamic_update_slice | solution.py:139
  177.1 8.8 %dynamic_update_slice.55 = bf16[1152,1152]{0,1:T(8,128)(2,1)S(1)} dynamic-update-slice(bf16[1152,1152]{0,1:T(8,128)(2,1)S(1)} %dynamic_update_slice.54, bf16[144,1152]{0,1:T(8,128)(2,1)S(1)} %copy.63, s32[]{:T(128)S(6)} %select_n.98, s32[]{:T(128)} %constant.180.clone.1) | dynamic-update-slice | bytes 663556 | tf_op jit(solution)/shard_map/dynamic_update_slice | solution.py:139
  213.9 17.3 %collective-permute-start = (bf16[512]{0:T(512)(128)(2,1)S(1)}, bf16[512]{0:T(512)(128)(2,1)S(1)}, u32[]{:S(2)}, u32[]{:S(2)}) collective-permute-start(bf16[512]{0:T(512)(128)(2,1)S(1)} %add_convert_fusion.1), channel_id=1, source_target_pairs={{0,4},{4,8},{8,12},{12,16},{16,20},{20,24},{24,28},{1,5},{5,9},{9,... | collective-permute-start | bytes 3080 | tf_op jit(solution)/shard_map/ppermute | solution.py:15
  232.6 7.5 collective-permute-start.12
  253.9 13.8 %collective-permute-done.14 = bf16[128,1152]{1,0:T(8,128)(2,1)S(1)} collective-permute-done((bf16[128,1152]{1,0:T(8,128)(2,1)S(1)}, bf16[128,1152]{1,0:T(8,128)(2,1)S(1)}, u32[]{:S(2)}, u32[]{:S(2)}) %collective-permute-start.14) | collective-permute-done | bytes 294944 | tf_op jit(solution)/shard_map/ppermute | solution.py:20
  309.7 9.2 %collective-permute-done.20 = bf16[128,1152]{1,0:T(8,128)(2,1)S(1)} collective-permute-done((bf16[128,1152]{1,0:T(8,128)(2,1)S(1)}, bf16[128,1152]{1,0:T(8,128)(2,1)S(1)}, u32[]{:S(2)}, u32[]{:S(2)}) %collective-permute-start.20) | collective-permute-done | bytes 294944 | tf_op jit(solution)/shard_map/ppermute | solution.py:20
  321.0 13.7 %collective-permute-start.22 = (bf16[128,1152]{1,0:T(8,128)(2,1)S(1)}, bf16[128,1152]{1,0:T(8,128)(2,1)S(1)}, u32[]{:S(2)}, u32[]{:S(2)}) collective-permute-start(bf16[128,1152]{1,0:T(8,128)(2,1)S(1)} %get-tuple-element.160), channel_id=1, source_target_pairs={{0,3},{1,0},{2,1},{3,2},{4,7},{5,4},{6,5},{7,6},{8,11},{9,8},{10,9... | collective-permute-start | bytes 884744 | tf_op jit(solution)/shard_map/ppermute | solution.py:20
  343.3 8.0 %multiply_convert_fusion = (bf16[512,1728]{0,1:T(8,128)(2,1)S(1)}, bf16[512,1728]{0,1:T(8,128)(2,1)S(1)}) fusion(f32[512,1728]{0,1:T(8,128)S(1)} %copy-done.81, f32[512,1728]{0,1:T(8,128)} %get-tuple-element.185, bf16[1728,1152]{0,1:T(8,128)(2,1)S(1)} %copy-done.71, bf16[128,1152]{1,0:T(8,128)(2,1)S(1)} %collective-permute-done.24, ...), kind=kOutput, calls=%fused_computation.20 | convolution fusion | flops 2064384000 | bytes 15777792 | tf_op jit(solution)/shard_map/ld,fd->lf/dot_general | solution.py:222
  393.8 7.3 collective-permute-done.26
  428.1 18.7 %collective-permute-done.31 = bf16[512,256]{1,0:T(8,128)(2,1)S(1)} collective-permute-done((bf16[512,256]{1,0:T(8,128)(2,1)S(1)}, bf16[512,256]{1,0:T(8,128)(2,1)S(1)}, u32[]{:S(2)}, u32[]{:S(2)}) %collective-permute-start.31) | collective-permute-done | bytes 262176 | tf_op jit(solution)/shard_map/ppermute | solution.py:15
  480.4 89.0 %reduce-scatter.15.cloned.1.call-done = bf16[144,1728]{1,0:T(8,128)(2,1)} async-done(((bf16[1152,1728]{1,0:T(8,128)(2,1)}), bf16[144,1728]{1,0:T(8,128)(2,1)}) %reduce-scatter.15.cloned.1.call-update) | async-done | bytes 497680
  571.7 88.6 %reduce-scatter.17.cloned.1.call-done = bf16[144,1728]{1,0:T(8,128)(2,1)} async-done(((bf16[1152,1728]{1,0:T(8,128)(2,1)}), bf16[144,1728]{1,0:T(8,128)(2,1)}) %reduce-scatter.17.cloned.1.call-update) | async-done | bytes 497680
  673.5 63.0 %reduce-scatter.19.cloned.1.call-done = bf16[144,1152]{1,0:T(8,128)(2,1)} async-done(((bf16[1152,1152]{1,0:T(8,128)(2,1)}), bf16[144,1152]{1,0:T(8,128)(2,1)}) %reduce-scatter.19.cloned.1.call-update) | async-done | bytes 331792
  744.9 9.7 %collective-permute-done.37 = bf16[144,640]{0,1:T(8,128)(2,1)S(1)} collective-permute-done((bf16[144,640]{0,1:T(8,128)(2,1)S(1)}, bf16[144,640]{0,1:T(8,128)(2,1)S(1)}, u32[]{:S(2)}, u32[]{:S(2)}) %collective-permute-start.37) | collective-permute-done | bytes 184352 | tf_op jit(solution)/shard_map/ppermute | solution.py:20
  (396 shorter events, 257.6 us)
Async XLA Ops:
  7.2 273.9 %all-gather.3.cloned.1.call-start = ((), (), s32[]{:S(2)}) async-start(), calls=%async_computation.4 | async-start | bytes 9289728 | tf_op jit(solution)/shard_map/all_gather | solution.py:141
  7.9 287.0 %all-gather.5.cloned.1.call-start = ((), (), s32[]{:S(2)}) async-start(), calls=%async_computation.5 | async-start | bytes 4644864 | tf_op jit(solution)/shard_map/all_gather | solution.py:142
  27.2 19.8 %collective-permute-start.2 = (bf16[144,1152]{1,0:T(8,128)(2,1)S(1)}, bf16[144,1152]{1,0:T(8,128)(2,1)S(1)}, u32[]{:S(2)}, u32[]{:S(2)}) collective-permute-start(bf16[144,1152]{1,0:T(8,128)(2,1)S(1)} %collective-permute-done.1), channel_id=1, source_target_pairs={{0,4},{4,8},{8,12},{12,16},{16,20},{20,24},{24,28},{28,0},{1,5},{5... | collective-permute-start | bytes 995336 | tf_op jit(solution)/shard_map/ppermute | solution.py:138
  47.0 19.5 %collective-permute-start.3 = (bf16[144,1152]{1,0:T(8,128)(2,1)S(1)}, bf16[144,1152]{1,0:T(8,128)(2,1)S(1)}, u32[]{:S(2)}, u32[]{:S(2)}) collective-permute-start(bf16[144,1152]{1,0:T(8,128)(2,1)S(1)} %collective-permute-done.2), channel_id=1, source_target_pairs={{0,4},{4,8},{8,12},{12,16},{16,20},{20,24},{24,28},{28,0},{1,5},{5... | collective-permute-start | bytes 995336 | tf_op jit(solution)/shard_map/ppermute | solution.py:138
  66.5 15.3 %collective-permute-start.4 = (bf16[144,1152]{1,0:T(8,128)(2,1)S(1)}, bf16[144,1152]{1,0:T(8,128)(2,1)S(1)}, u32[]{:S(2)}, u32[]{:S(2)}) collective-permute-start(bf16[144,1152]{1,0:T(8,128)(2,1)S(1)} %collective-permute-done.3), channel_id=1, source_target_pairs={{0,4},{4,8},{8,12},{12,16},{16,20},{20,24},{24,28},{28,0},{1,5},{5... | collective-permute-start | bytes 995336 | tf_op jit(solution)/shard_map/ppermute | solution.py:138
  81.8 17.5 %collective-permute-start.5 = (bf16[144,1152]{1,0:T(8,128)(2,1)S(1)}, bf16[144,1152]{1,0:T(8,128)(2,1)}, u32[]{:S(2)}, u32[]{:S(2)}) collective-permute-start(bf16[144,1152]{1,0:T(8,128)(2,1)S(1)} %collective-permute-done.4), channel_id=1, source_target_pairs={{0,4},{4,8},{8,12},{12,16},{16,20},{20,24},{24,28},{28,0},{1,5},{5... | collective-permute-start | bytes 995336 | tf_op jit(solution)/shard_map/ppermute | solution.py:138
  99.3 18.9 %collective-permute-start.6 = (bf16[144,1152]{1,0:T(8,128)(2,1)}, bf16[144,1152]{1,0:T(8,128)(2,1)}, u32[]{:S(2)}, u32[]{:S(2)}) collective-permute-start(bf16[144,1152]{1,0:T(8,128)(2,1)} %collective-permute-done.5), channel_id=1, source_target_pairs={{0,4},{4,8},{8,12},{12,16},{16,20},{20,24},{24,28},{28,0},{1,5},{5... | collective-permute-start | bytes 995336 | tf_op jit(solution)/shard_map/ppermute | solution.py:138
  118.2 57.6 %collective-permute-start.7 = (bf16[144,1152]{1,0:T(8,128)(2,1)}, bf16[144,1152]{1,0:T(8,128)(2,1)}, u32[]{:S(2)}, u32[]{:S(2)}) collective-permute-start(bf16[144,1152]{1,0:T(8,128)(2,1)} %collective-permute-done.6), channel_id=1, source_target_pairs={{0,4},{4,8},{8,12},{12,16},{16,20},{20,24},{24,28},{28,0},{1,5},{5... | collective-permute-start | bytes 995336 | tf_op jit(solution)/shard_map/ppermute | solution.py:138
  189.6 288.5 %reduce-scatter.13.cloned.1.call-start = ((), (), s32[]{:S(2)}) async-start(), calls=%async_computation.6 | async-start | bytes 4644864
  190.2 14.5 %collective-permute-start.9 = (bf16[128,1152]{1,0:T(8,128)(2,1)}, bf16[128,1152]{1,0:T(8,128)(2,1)S(1)}, u32[]{:S(2)}, u32[]{:S(2)}) collective-permute-start(bf16[128,1152]{1,0:T(8,128)(2,1)} %get-tuple-element.141), channel_id=1, source_target_pairs={{0,2},{1,3},{2,0},{3,1},{4,6},{5,7},{6,4},{7,5},{8,10},{9,11},{10,... | collective-permute-start | bytes 884744 | tf_op jit(solution)/shard_map/ppermute | solution.py:20
  211.5 28.6 %collective-permute-start.11 = (bf16[512,256]{1,0:T(8,128)(2,1)S(1)}, bf16[512,256]{1,0:T(8,128)(2,1)S(1)}, u32[]{:S(2)}, u32[]{:S(2)}) collective-permute-start(bf16[512,256]{1,0:T(8,128)(2,1)S(1)} %pad_maximum_fusion.9), channel_id=1, source_target_pairs={{0,4},{4,8},{8,12},{12,16},{16,20},{20,24},{24,28},{1,5},{5,9},{9,... | collective-permute-start | bytes 786440 | tf_op jit(solution)/shard_map/ppermute | solution.py:15
  213.9 18.6 %collective-permute-start = (bf16[512]{0:T(512)(128)(2,1)S(1)}, bf16[512]{0:T(512)(128)(2,1)S(1)}, u32[]{:S(2)}, u32[]{:S(2)}) collective-permute-start(bf16[512]{0:T(512)(128)(2,1)S(1)} %add_convert_fusion.1), channel_id=1, source_target_pairs={{0,4},{4,8},{8,12},{12,16},{16,20},{20,24},{24,28},{1,5},{5,9},{9,... | collective-permute-start | bytes 3080 | tf_op jit(solution)/shard_map/ppermute | solution.py:15
  248.6 19.0 %collective-permute-start.14 = (bf16[128,1152]{1,0:T(8,128)(2,1)S(1)}, bf16[128,1152]{1,0:T(8,128)(2,1)S(1)}, u32[]{:S(2)}, u32[]{:S(2)}) collective-permute-start(bf16[128,1152]{1,0:T(8,128)(2,1)S(1)} %get-tuple-element.159), channel_id=1, source_target_pairs={{0,2},{1,3},{2,0},{3,1},{4,6},{5,7},{6,4},{7,5},{8,10},{9,11},{10,... | collective-permute-start | bytes 884744 | tf_op jit(solution)/shard_map/ppermute | solution.py:20
  302.7 16.3 %collective-permute-start.20 = (bf16[128,1152]{1,0:T(8,128)(2,1)S(1)}, bf16[128,1152]{1,0:T(8,128)(2,1)S(1)}, u32[]{:S(2)}, u32[]{:S(2)}) collective-permute-start(bf16[128,1152]{1,0:T(8,128)(2,1)S(1)} %get-tuple-element.156), channel_id=1, source_target_pairs={{0,2},{1,3},{2,0},{3,1},{4,6},{5,7},{6,4},{7,5},{8,10},{9,11},{10,... | collective-permute-start | bytes 884744 | tf_op jit(solution)/shard_map/ppermute | solution.py:20
  321.0 17.9 %collective-permute-start.22 = (bf16[128,1152]{1,0:T(8,128)(2,1)S(1)}, bf16[128,1152]{1,0:T(8,128)(2,1)S(1)}, u32[]{:S(2)}, u32[]{:S(2)}) collective-permute-start(bf16[128,1152]{1,0:T(8,128)(2,1)S(1)} %get-tuple-element.160), channel_id=1, source_target_pairs={{0,3},{1,0},{2,1},{3,2},{4,7},{5,4},{6,5},{7,6},{8,11},{9,8},{10,9... | collective-permute-start | bytes 884744 | tf_op jit(solution)/shard_map/ppermute | solution.py:20
  374.9 194.5 %reduce-scatter.15.cloned.1.call-start = ((), (), s32[]{:S(2)}) async-start(), calls=%async_computation.7 | async-start | bytes 4644864
  381.4 278.8 %reduce-scatter.17.cloned.1.call-start = ((), (), s32[]{:S(2)}) async-start(), calls=%async_computation.8 | async-start | bytes 4644864
  385.4 15.7 %collective-permute-start.26 = (bf16[128,1152]{1,0:T(8,128)(2,1)}, bf16[128,1152]{1,0:T(8,128)(2,1)}, u32[]{:S(2)}, u32[]{:S(2)}) collective-permute-start(bf16[128,1152]{1,0:T(8,128)(2,1)} %get-tuple-element.153), channel_id=1, source_target_pairs={{0,2},{1,3},{2,0},{3,1},{4,6},{5,7},{6,4},{7,5},{8,10},{9,11},{10,... | collective-permute-start | bytes 884744 | tf_op jit(solution)/shard_map/ppermute | solution.py:20
  393.7 342.8 %reduce-scatter.19.cloned.1.call-start = ((), (), s32[]{:S(2)}) async-start(), calls=%async_computation.9 | async-start | bytes 2985984
  421.4 27.7 %collective-permute-start.32 = (bf16[512,256]{1,0:T(8,128)(2,1)S(1)}, bf16[512,256]{1,0:T(8,128)(2,1)S(1)}, u32[]{:S(2)}, u32[]{:S(2)}) collective-permute-start(bf16[512,256]{1,0:T(8,128)(2,1)S(1)} %slice.319), channel_id=1, source_target_pairs={{4,0},{8,4},{12,8},{16,12},{20,16},{24,20},{28,24},{5,1},{9,5},{13... | collective-permute-start | bytes 786440 | tf_op jit(solution)/shard_map/ppermute | solution.py:15
  424.9 21.9 %collective-permute-start.31 = (bf16[512,256]{1,0:T(8,128)(2,1)S(1)}, bf16[512,256]{1,0:T(8,128)(2,1)S(1)}, u32[]{:S(2)}, u32[]{:S(2)}) collective-permute-start(bf16[512,256]{1,0:T(8,128)(2,1)S(1)} %slice.320), channel_id=1, source_target_pairs={{4,0},{8,4},{12,8},{16,12},{20,16},{24,20},{28,24},{5,1},{9,5},{13... | collective-permute-start | bytes 786440 | tf_op jit(solution)/shard_map/ppermute | solution.py:15
  450.9 15.1 %collective-permute-start.34 = (bf16[128,1152]{1,0:T(8,128)(2,1)S(1)}, bf16[128,1152]{1,0:T(8,128)(2,1)S(1)}, u32[]{:S(2)}, u32[]{:S(2)}) collective-permute-start(bf16[128,1152]{1,0:T(8,128)(2,1)S(1)} %get-tuple-element.150), channel_id=1, source_target_pairs={{0,2},{1,3},{2,0},{3,1},{4,6},{5,7},{6,4},{7,5},{8,10},{9,11},{10,... | collective-permute-start | bytes 884744 | tf_op jit(solution)/shard_map/ppermute | solution.py:20
  737.7 16.8 %collective-permute-start.37 = (bf16[144,640]{0,1:T(8,128)(2,1)S(1)}, bf16[144,640]{0,1:T(8,128)(2,1)S(1)}, u32[]{:S(2)}, u32[]{:S(2)}) collective-permute-start(bf16[144,640]{0,1:T(8,128)(2,1)S(1)} %copy.85), channel_id=1, source_target_pairs={{0,2},{1,3},{2,0},{3,1},{4,6},{5,7},{6,4},{7,5},{8,10},{9,11},{10,... | collective-permute-start | bytes 552968 | tf_op jit(solution)/shard_map/ppermute | solution.py:20
  739.2 15.5 %collective-permute-start.36 = (bf16[144,640]{0,1:T(8,128)(2,1)S(1)}, bf16[144,640]{0,1:T(8,128)(2,1)S(1)}, u32[]{:S(2)}, u32[]{:S(2)}) collective-permute-start(bf16[144,640]{0,1:T(8,128)(2,1)S(1)} %copy.85), channel_id=1, source_target_pairs={{0,1},{1,2},{2,3},{3,0},{4,5},{5,6},{6,7},{7,4},{8,9},{9,10},{10,1... | collective-permute-start | bytes 552968 | tf_op jit(solution)/shard_map/ppermute | solution.py:20
  (107 other events, 1163.8 us)
Sparse Core Ops, SparseCore 0:
  10.2 164.6 all-gather.2
  189.7 94.0 all-gather.4
  375.0 103.0 reduce-scatter.12
  481.9 87.4 reduce-scatter.14
  572.8 87.3 reduce-scatter.16
  665.9 70.5 reduce-scatter.18
